TPU v7x, 32 devices: a whole 2x2x4 slice. The times are simulated.
32 devices in a mesh: chan: 8 (over y, x, core), tm: 4 (over z).
Axes of the slice: x: 2, y: 2, z: 4, core: 2. Of those that a mesh axis runs over, the one named last changes fastest.
Arguments:
- records: bfloat16 [128, 16384], P('chan', 'tm'), may hold values from -100 to 100, as said below
- pair_rows: int32 [8, 16], P('chan'), may hold values from 0 to 15, each once within a row
- fir_taps: float32 [32], replicated, may hold values from -1 to 1
- source_blocks: int32 [2], replicated, may hold values from 0 to 15
Outputs:
- stacks: float32 [2, 8, 128, 1024], P(None, None, 'chan', 'tm')
Inputs may be any that keep to these rules, and one draw needn't show every extreme that they name: Seismic noise records, one row a channel.
All inputs are finite; a program needn't handle non-finite values.
Results may differ from a plain program's by a relative error of at most 0.0037.
Values may be sent and summed in bfloat16 or wider, within the bound.
A program may use at most 128 MiB of HBM per device.

v0:
```python
import math

import jax
import jax.numpy as jnp
from jax import lax
from jax.sharding import PartitionSpec as P

VS = 8
STEPS = 2


def from_partner(block, axis, apart):
    count = lax.axis_size(axis)
    route = []
    for low in range(count):
        high = low | 1 << apart
        if high != low and high < count:
            route += [(low, high), (high, low)]
    return lax.ppermute(block, axis, route)


def passed_along(x, axis, by):
    count = lax.axis_size(axis)
    pairs = [(i, i + by) for i in range(count) if 0 <= i + by < count]
    return lax.ppermute(x, axis, pairs)


def broadcast(block, axis, owner):
    block = jnp.where(lax.axis_index(axis) == owner, block, jnp.zeros_like(block))
    return lax.psum(block, axis)


def skewed_tile(window, first, seg_len, lag_block):
    shifted = [
        lax.slice_in_dim(window, first + k, first + k + seg_len, 1, 1) for k in range(lag_block)
    ]
    return jnp.stack(shifted, axis=1)


def correlate(receiver, source_ext, seg_len):
    recv_count, total_len = receiver.shape
    lag_count = source_ext.shape[1] - total_len
    lag_block = min(128, lag_count)
    seg_count = total_len // seg_len
    source_count = source_ext.shape[0]

    def one_segment(stack_sum, segment):
        lag_parts = []
        for lag_start in range(0, lag_count, lag_block):
            first = lag_count - lag_start - lag_block + 1
            tile_rows = skewed_tile(source_ext, first, seg_len, lag_block)
            product = jnp.einsum(
                "cu,rku->rck", receiver, tile_rows, preferred_element_type=jnp.float32
            )
            lag_parts.append(jnp.flip(product, axis=2))
        return (stack_sum + jnp.concatenate(lag_parts, axis=2), None)

    zero_stack = jnp.zeros((source_count, recv_count, lag_count), jnp.float32)
    stack_sum, _ = lax.scan(one_segment, zero_stack, jnp.arange(seg_count))
    return stack_sum


def shards(records, pair_rows, fir_taps, source_blocks):
    flip_bit = lax.axis_size("chan").bit_length() - 2
    partner_raw = from_partner(records, "chan", flip_bit)
    partner = jnp.take(partner_raw, pair_rows[0], axis=0)
    combined = 0.5 * (records.astype(jnp.float32) + partner.astype(jnp.float32))
    tap_count = fir_taps.shape[0]
    tail_rows = passed_along(combined[:, -tap_count:], "tm", 1)
    extended = jnp.concatenate([tail_rows, combined], axis=1)
    samples = records.shape[1] // 4
    filtered = jnp.zeros((records.shape[0], samples), jnp.float32)
    for offset in range(tap_count):
        begin = tap_count + 3 - offset
        filtered = filtered + fir_taps[offset] * extended[:, begin : begin + 4 * samples : 4]
    window_len = samples * lax.axis_size("tm")
    row_total = lax.psum(jnp.sum(filtered * filtered, axis=1), "tm")
    power = row_total / window_len
    whitened = (filtered * lax.rsqrt(power + 1e-06)[:, None]).astype(jnp.bfloat16)
    per_device = whitened.shape[0] // VS
    gathered = []
    for step_index in range(STEPS):
        owner_index = source_blocks[step_index] // per_device
        within = source_blocks[step_index] % per_device
        own_rows = lax.dynamic_slice_in_dim(whitened, within * VS, VS, 0)
        gathered.append(broadcast(own_rows, "chan", owner_index))
    sources = jnp.stack(gathered)
    scale_factor = 1.0 / math.sqrt(window_len)
    source_tail = passed_along(sources, "tm", 1)
    extended_src = jnp.concatenate([source_tail, sources], axis=2)
    partial_stacks = jnp.stack(
        [correlate(whitened, extended_src[step_index], samples) for step_index in range(STEPS)]
    )
    stacks = lax.psum_scatter(partial_stacks, "tm", scatter_dimension=3, tiled=True)
    return stacks * scale_factor


def solution(mesh):
    return jax.shard_map(
        shards,
        mesh=mesh,
        in_specs=(P("chan", "tm"), P("chan", None), P(), P()),
        out_specs=P(None, None, "chan", "tm"),
        check_vma=False,
    )
```

profile of v0, /device:TPU:0, one launch (start us, length us, event | category | flops | bytes accessed | tf_op | source)
XLA Modules:
  0.0 759.4 jit_solution(17234330818454927625)
XLA Ops:
  6.5 3.0 collective-permute-start
  12.2 1.8 fusion.29
  18.1 2.1 fusion.28
  21.9 3.5 collective-permute-start.1
  26.1 2.2 slice.8409
  28.3 2.2 slice.8407
  30.6 2.2 slice.8405
  32.8 2.2 slice.8403
  35.1 2.2 slice.8466
  37.4 2.2 slice.8464
  39.6 2.2 slice.8462
  41.8 2.5 slice.8460
  44.3 2.2 slice.8458
  46.6 2.2 slice.8456
  48.8 2.2 slice.8454
  51.0 2.2 slice.8452
  53.2 2.2 slice.8450
  55.4 2.2 slice.8448
  57.7 2.2 slice.8446
  59.9 2.4 slice.8444
  62.3 2.2 slice.8442
  64.5 2.2 slice.8440
  66.7 2.2 slice.8438
  68.9 2.2 slice.8436
  71.1 2.2 slice.8434
  73.4 2.2 slice.8432
  75.6 2.2 slice.8430
  77.8 2.6 slice.8428
  80.4 2.2 slice.8426
  82.6 2.2 slice.8424
  84.8 2.2 slice.8422
  87.1 2.2 slice.8420
  89.3 2.2 slice.8418
  91.5 2.2 slice.8416
  93.7 2.2 slice.8414
  95.9 2.4 slice.8412
  98.3 20.2 %multiply_reduce_fusion = (f32[16]{0:T(128)S(1)}, f32[16,1024]{1,0:T(8,128)S(1)}) fusion(f32[16,1024]{1,0:T(8,128)S(1)} %slice.8466, f32[]{:T(128)} %bitcast.35, f32[16,1024]{1,0:T(8,128)S(1)} %slice.8464, f32[]{:T(128)} %bitcast.34, f32[16,1024]{1,0:T(8,128)S(1)} %slice.8462, f32[]{:T(128)} %bitcast.33, f32[16,1024]{1,0:T(8,128)S(1)} %slice.8460, ...), kind=kLoop, calls=%fused_computation.1955 | loop fusion | flops 1064944 | bytes 2162880 | tf_op jit(solution)/shard_map/reduce_sum | solution.py:77
  118.5 9.9 %psum.21 = f32[16]{0:T(128)S(1)} all-reduce(f32[16]{0:T(128)S(1)} %get-tuple-element.25), channel_id=1, replica_groups=mesh['chan'=8,'tm'=4] {'tm'}, use_global_device_ids=true, to_apply=%region_1.2 | all-reduce | flops 16 | bytes 128 | tf_op jit(solution)/shard_map/psum | solution.py:77
  128.6 22.4 %all-reduce = (bf16[1,8,1024]{2,1,0:T(8,128)(2,1)S(1)}, bf16[1,8,1024]{2,1,0:T(8,128)(2,1)S(1)}) all-reduce(bf16[1,8,1024]{2,1,0:T(8,128)(2,1)S(1)} %get-tuple-element.164, bf16[1,8,1024]{2,1,0:T(8,128)(2,1)S(1)} %get-tuple-element.163), channel_id=1, replica_groups=mesh['chan'=8,'tm'=4] {'chan'}, use_global_device_ids=true, to_apply=%region_2.3 | all-reduce | flops 16384 | bytes 65536 | tf_op jit(solution)/shard_map/psum | solution.py:30
  151.0 2.5 collective-permute-start.2
  223.1 16.8 %stack.8405 = bf16[8,128,1024]{2,1,0:T(8,128)(2,1)S(1)} concatenate(bf16[8,1,1024]{2,1,0:T(2,128)(2,1)S(1)} %copy.4543, bf16[8,1,1024]{2,1,0:T(2,128)(2,1)S(1)} %copy.4544, bf16[8,1,1024]{2,1,0:T(2,128)(2,1)S(1)} %copy.4545, bf16[8,1,1024]{2,1,0:T(2,128)(2,1)S(1)} %copy.4546, bf16[8,1,1024]{2,1,0:T(2,128)(2,1)S(1)} %copy.4547, bf16[8,1,1024]{2,1,0:T(2,128)(2,1)S(1)} %copy.4548, ...), dimensions={1} | concatenate | bytes 4194304 | tf_op jit(solution)/shard_map/while/body/eval_jaxpr/stack | solution.py:37
  446.5 2.3 fusion.17
  546.8 2.3 fusion.21
  635.7 2.4 convolution_bitcast_fusion
  659.6 2.4 convolution_bitcast_fusion.1
  683.3 2.4 convolution_bitcast_fusion.3
  708.1 2.4 convolution_bitcast_fusion.5
  725.0 25.4 %reduce-scatter.2.cloned.1.call-done = f32[2,8,16,256]{3,2,1,0:T(8,128)} async-done(((f32[2,8,16,1024]{3,2,1,0:T(8,128)}), f32[2,8,16,256]{3,2,1,0:T(8,128)}) %reduce-scatter.2.cloned.1.call-update) | async-done | bytes 262160 | tf_op jit(solution)/shard_map/reduce_scatter | solution.py:94
  (2176 shorter events, 544.9 us)
Async XLA Ops:
  6.5 743.9 %reduce-scatter.2.cloned.1.call-start = ((), (), s32[]{:S(2)}) async-start(), calls=%async_computation.1 | async-start | bytes 1310720 | tf_op jit(solution)/shard_map/reduce_scatter | solution.py:94
  6.5 13.7 %collective-permute-start = (bf16[16,4096]{1,0:T(8,128)(2,1)}, bf16[16,4096]{1,0:T(8,128)(2,1)S(1)}, u32[]{:S(2)}, u32[]{:S(2)}) collective-permute-start(bf16[16,4096]{1,0:T(8,128)(2,1)} %param.4), channel_id=1, source_target_pairs={{0,16},{16,0},{4,20},{20,4},{8,24},{24,8},{12,28},{28,12},{1,17},{... | collective-permute-start | bytes 393224 | tf_op jit(solution)/shard_map/ppermute | solution.py:19
  21.9 13.0 %collective-permute-start.1 = (f32[16,32]{1,0:T(8,128)S(1)}, f32[16,32]{1,0:T(8,128)S(1)}, u32[]{:S(2)}, u32[]{:S(2)}) collective-permute-start(f32[16,32]{1,0:T(8,128)S(1)} %slice.10520), channel_id=1, source_target_pairs={{0,1},{1,2},{2,3},{4,5},{5,6},{6,7},{8,9},{9,10},{10,11},{12,13},{... | collective-permute-start | bytes 6152 | tf_op jit(solution)/shard_map/ppermute | solution.py:25
  151.0 4.1 collective-permute-start.2
  240.6 85.8 %copy-start.13 = (bf16[8,128,1024]{2,0,1:T(8,128)(2,1)S(1)}, bf16[8,128,1024]{2,0,1:T(8,128)(2,1)}, u32[]{:S(2)}) copy-start(bf16[8,128,1024]{2,0,1:T(8,128)(2,1)} %constant_dynamic-update-slice_fusion.769) | copy-start | bytes 6291460
  325.0 11.2 %copy-start.12 = (bf16[8,128,1024]{2,0,1:T(8,128)(2,1)S(1)}, bf16[8,128,1024]{2,0,1:T(8,128)(2,1)}, u32[]{:S(2)}) copy-start(bf16[8,128,1024]{2,0,1:T(8,128)(2,1)} %constant_dynamic-update-slice_fusion.641) | copy-start | bytes 6291460
  348.5 85.9 %copy-start.11 = (bf16[8,128,1024]{2,0,1:T(8,128)(2,1)S(1)}, bf16[8,128,1024]{2,0,1:T(8,128)(2,1)}, u32[]{:S(2)}) copy-start(bf16[8,128,1024]{2,0,1:T(8,128)(2,1)} %constant_dynamic-update-slice_fusion.385) | copy-start | bytes 6291460
  449.0 85.8 %copy-start.10 = (bf16[8,128,1024]{2,0,1:T(8,128)(2,1)S(1)}, bf16[8,128,1024]{2,0,1:T(8,128)(2,1)}, u32[]{:S(2)}) copy-start(bf16[8,128,1024]{2,0,1:T(8,128)(2,1)} %constant_dynamic-update-slice_fusion.129) | copy-start | bytes 6291460
  635.7 2.6 copy-start.8
  638.3 9.8 %copy-start.7 = (bf16[8,128,1024]{2,0,1:T(8,128)(2,1)S(1)}, bf16[8,128,1024]{2,0,1:T(8,128)(2,1)}, u32[]{:S(2)}) copy-start(bf16[8,128,1024]{2,0,1:T(8,128)(2,1)} %constant_dynamic-update-slice_fusion.1673) | copy-start | bytes 6291460
  658.2 1.4 copy-start.9
  659.6 2.7 copy-start.5
  662.2 9.8 %copy-start.4 = (bf16[8,128,1024]{2,0,1:T(8,128)(2,1)S(1)}, bf16[8,128,1024]{2,0,1:T(8,128)(2,1)}, u32[]{:S(2)}) copy-start(bf16[8,128,1024]{2,0,1:T(8,128)(2,1)} %constant_dynamic-update-slice_fusion.1417) | copy-start | bytes 6291460
  681.9 1.4 copy-start.6
  683.3 3.3 copy-start.2
  686.6 9.8 %copy-start.1 = (bf16[8,128,1024]{2,0,1:T(8,128)(2,1)S(1)}, bf16[8,128,1024]{2,0,1:T(8,128)(2,1)}, u32[]{:S(2)}) copy-start(bf16[8,128,1024]{2,0,1:T(8,128)(2,1)} %constant_dynamic-update-slice_fusion.1161) | copy-start | bytes 6291460
  706.2 1.8 copy-start.3
  708.1 3.3 copy-start
  711.4 9.8 %copy-start.14 = (bf16[8,128,1024]{2,0,1:T(8,128)(2,1)S(1)}, bf16[8,128,1024]{2,0,1:T(8,128)(2,1)}, u32[]{:S(2)}) copy-start(bf16[8,128,1024]{2,0,1:T(8,128)(2,1)} %constant_dynamic-update-slice_fusion.771) | copy-start | bytes 6291460
  722.5 1.0 copy-start.15
  722.6 1.0 copy-start.23
  722.6 1.0 copy-start.24
  722.6 1.1 copy-start.21
  722.6 1.1 copy-start.22
  722.6 1.1 copy-start.19
  722.6 1.1 copy-start.20
  722.6 1.1 copy-start.17
  722.6 1.1 copy-start.18
  722.6 1.2 copy-start.16
Sparse Core Ops, SparseCore 0:
  725.1 25.2 reduce-scatter.1
where the time goes:
time: 770 us; the launch traced here: 759 us
  local copies, waits for them, and re-layouts  624 us (81%)
  blocking collectives  32.3 us (4%)
  waiting for transfers between devices  27.1 us (4%)
  other arithmetic  25.5 us (3%)
  matrix products  21.1 us (3%)
  between operations  20.7 us (3%)
  starting transfers between devices  8.97 us (1%)
    unnamed x1970, local copies, waits for them, and re-layouts  460 us
    another operation x144, local copies, waits for them, and re-layouts, skewed_tile(): return jnp.stack(shifted, axis=1)  76.1 us
    slice x32, local copies, waits for them, and re-layouts, shards(): extended[:, begin:begin + 4 * samples:4]  71.9 us
    reduce_scatter x1, waiting for transfers between devices, shards(): lax.psum_scatter(partial_stacks, 'tm', scatter_dimension=3, tiled=True)  25.4 us
    psum x1, blocking collectives, broadcast(): return lax.psum(block, axis)  22.4 us
    dot_general x16, matrix products, one_segment(): jnp.einsum('cu,rku->rck', receiver, tile_rows, preferred_element_type=jnp...  21.1 us
    reduce_sum x1, other arithmetic, shards(): row_total = lax.psum(jnp.sum(filtered * filtered, axis=1), 'tm')  20.2 us
  transfers between devices with their start and end apart: 4, of which 2 were waited for; matrix products, arithmetic and copies ran while one was open for 2% of the time, Pallas kernels for 0%

commit v1 on v0

v1 whole, which is shorter than its diff:
```python
import functools
import math

import jax
import jax.numpy as jnp
from jax import lax
from jax.experimental import pallas as pl
from jax.experimental.pallas import tpu as pltpu
from jax.sharding import PartitionSpec as P

VS = 8
STEPS = 2
LAGS = 1024
TAPS = 32
LANES = 128
FINE = 16


def body(C, T, rows, taps_ref, pair_ref, blocks_ref, rec_ref, out_ref,
         halo, filt, pfilt, pw, chw, tw, ts, sp, wp,
         halo_s, halo_r, part_s, part_r, pw_s, pw_r, ch_s, ch_r, tw_s, tw_r, ts_s, ts_r):
    me = lax.axis_index("chan")
    t = lax.axis_index("tm")
    f32, bf16 = jnp.float32, jnp.bfloat16
    samples = rec_ref.shape[1] // 4
    lag_dev = LAGS // T
    P_ = max(1, lag_dev // LANES)
    A_ = min(lag_dev, LANES) // FINE
    window = samples * T

    def at_chan(d):
        return lax.rem(me + d, C)

    def at_tm(d):
        return lax.rem(t + d, T)

    barrier = pltpu.get_barrier_semaphore()
    for d in range(1, C):
        pl.semaphore_signal(barrier, inc=1, device_id={"chan": at_chan(d)}, device_id_type=pl.DeviceIdType.MESH)
    for d in range(1, T):
        pl.semaphore_signal(barrier, inc=1, device_id={"tm": at_tm(d)}, device_id_type=pl.DeviceIdType.MESH)

    def remote(src, dst, ssem, rsem, where):
        return pltpu.make_async_remote_copy(
            src_ref=src, dst_ref=dst, send_sem=ssem, recv_sem=rsem,
            device_id=where, device_id_type=pl.DeviceIdType.MESH)

    group = 4 * LANES
    depth = LANES + group
    j = lax.broadcasted_iota(jnp.int32, (depth, LANES), 0)
    n = lax.broadcasted_iota(jnp.int32, (depth, LANES), 1)
    tap = 4 * n + 3 - (j - LANES)
    band = jnp.zeros((depth, LANES), f32)
    for k in range(TAPS):
        band = jnp.where(tap == k, taps_ref[k], band)
    hi = band.astype(bf16)
    lo = (band - hi.astype(f32)).astype(bf16)
    band2 = jnp.concatenate([hi, lo], axis=1)

    pl.semaphore_wait(barrier, C + T - 2)
    tail = rec_ref.shape[1] - LANES
    halo_copy = remote(rec_ref.at[:, pl.ds(tail, LANES)], halo, halo_s, halo_r, {"tm": at_tm(1)})
    halo_copy.start()

    sp[:, :LANES] = jnp.zeros((rows, LANES), f32)
    wp[:, window:] = jnp.zeros((rows, wp.shape[1] - window), f32)

    groups = samples // LANES
    parts = []
    for g in range(groups):
        if g == 0:
            first = jnp.zeros((rows, LANES), bf16)
        else:
            first = rec_ref[:, group * g - LANES:group * g]
        parts.append(jnp.concatenate([first, rec_ref[:, group * g:group * (g + 1)]], axis=1))
    lhs = jnp.concatenate(parts, axis=0)
    both = jnp.dot(lhs, band2, preferred_element_type=f32)
    res = both[:, :LANES] + both[:, LANES:]
    halo_copy.wait()
    edge = jnp.dot(halo[...], band2[:LANES], preferred_element_type=f32)
    edge = edge[:, :LANES] + edge[:, LANES:]
    edge = jnp.where(t > 0, edge, jnp.zeros_like(edge))
    for g in range(groups):
        piece = res[rows * g:rows * (g + 1)]
        if g == 0:
            piece = piece + edge
        filt[:, LANES * g:LANES * (g + 1)] = piece
    part_copy = remote(filt, pfilt, part_s, part_r, {"chan": at_chan(C // 2)})
    part_copy.start()
    rr = lax.broadcasted_iota(jnp.int32, (rows, rows), 0)
    cc = lax.broadcasted_iota(jnp.int32, (rows, rows), 1)
    pick = jnp.zeros((rows, rows), jnp.int32)
    for r in range(rows):
        pick = jnp.where(rr == r, pair_ref[0, r], pick)
    perm = jnp.where(pick == cc, 1.0, 0.0).astype(f32)
    part_copy.wait()
    filtered = 0.5 * (filt[...] + jnp.dot(perm, pfilt[...], precision=lax.Precision.HIGHEST,
                                          preferred_element_type=f32))
    sq = filtered * filtered
    acc = sq[:, :LANES]
    for g in range(1, groups):
        acc = acc + sq[:, LANES * g:LANES * (g + 1)]
    pw[t] = acc

    def spread(buf, slot, ssem, rsem, count, axis, place):
        sends = [remote(buf.at[slot], buf.at[slot], ssem.at[d], rsem.at[d], {axis: place(d)})
                 for d in range(1, count)]
        for s in sends:
            s.start()
        return sends

    def arrive(buf, ssem, rsem, count, axis, place):
        for d in range(1, count):
            slot = place(count - d)
            remote(buf.at[slot], buf.at[slot], ssem.at[d], rsem.at[d], {axis: place(d)}).wait_recv()

    pw_sends = spread(pw, t, pw_s, pw_r, T, "tm", at_tm)
    arrive(pw, pw_s, pw_r, T, "tm", at_tm)
    total = pw[0]
    for i in range(1, T):
        total = total + pw[i]
    power = jnp.sum(total, axis=1, keepdims=True) / window
    white = (filtered * lax.rsqrt(power + 1e-6)).astype(bf16)
    chw[me] = white
    tw[t] = white
    ch_sends = spread(chw, me, ch_s, ch_r, C, "chan", at_chan)
    tw_sends = spread(tw, t, tw_s, tw_r, T, "tm", at_tm)

    arrive(chw, ch_s, ch_r, C, "chan", at_chan)
    picked = []
    per = rows // VS
    for step in range(STEPS):
        blk = blocks_ref[step]
        owner = lax.div(blk, per)
        within = lax.rem(blk, per)
        x = chw[owner].astype(f32)
        half = x[:VS]
        for q in range(1, per):
            half = jnp.where(within == q, x[VS * q:VS * (q + 1)], half)
        picked.append(half)
    ts[t] = jnp.concatenate(picked, axis=0).astype(bf16)
    ts_sends = spread(ts, t, ts_s, ts_r, T, "tm", at_tm)
    arrive(tw, tw_s, tw_r, T, "tm", at_tm)
    for i in range(T):
        wp[:, samples * i:samples * (i + 1)] = tw[i].astype(f32)
    arrive(ts, ts_s, ts_r, T, "tm", at_tm)
    for i in range(T):
        sp[:, LANES + samples * i:LANES + samples * (i + 1)] = ts[i].astype(f32)

    lag0 = t * lag_dev
    wide = samples + LANES * P_
    if lag_dev % LANES == 0:
        base, rest = lag0, 0
    else:
        base = lax.div(lag0, LANES) * LANES
        rest = lax.rem(lag0, LANES)

    def block(i, z):
        s0 = pl.multiple_of(i * samples, LANES)
        w0 = pl.multiple_of(i * samples + base, LANES)
        srows = sp[:, pl.ds(s0, samples + LANES)]
        wrows = wp[:, pl.ds(w0, wide)]
        xs = []
        for s in range(STEPS * VS):
            one = jnp.broadcast_to(srows[s:s + 1], (FINE, samples + LANES))
            xs.append(pltpu.roll(one, 0, 1, stride=1, stride_axis=0)[:, LANES:].astype(bf16))
        rolled = []
        for a in range(A_):
            if lag_dev % LANES == 0:
                sh = (wide - FINE * a) % wide
            else:
                sh = wide - FINE * a - rest
            rolled.append(pltpu.roll(wrows, sh, 1) if not (isinstance(sh, int) and sh == 0) else wrows)
        ws = [rolled[a][:, LANES * p:LANES * p + samples].astype(bf16)
              for p in range(P_) for a in range(A_)]
        return z + lax.dot_general(jnp.concatenate(ws, axis=0), jnp.concatenate(xs, axis=0),
                                   (((1,), (1,)), ((), ())), preferred_element_type=f32)

    z = lax.fori_loop(0, T, block, jnp.zeros((P_ * A_ * rows, STEPS * VS * FINE), f32))
    z = z * (1.0 / math.sqrt(window))

    lane_group = lax.broadcasted_iota(jnp.int32, (rows, LANES), 1) // FINE
    per_tile = LANES // FINE
    width = min(lag_dev, LANES)
    for p in range(P_):
        for s in range(STEPS * VS):
            lo_s = s // per_tile * LANES
            o = None
            for a in range(A_):
                r0 = (p * A_ + a) * rows
                tile = z[r0:r0 + rows, lo_s:lo_s + LANES]
                sh = (FINE * (a - s % per_tile)) % LANES
                if sh:
                    tile = pltpu.roll(tile, sh, 1)
                o = tile if o is None else jnp.where(lane_group == a, tile, o)
            out_ref[s, :, LANES * p:LANES * p + width] = o[:, :width]

    for s in pw_sends + ch_sends + tw_sends + ts_sends:
        s.wait_send()


def shards(records, pair_rows, fir_taps, source_blocks):
    C = lax.axis_size("chan")
    T = lax.axis_size("tm")
    rows, raw = records.shape
    samples = raw // 4
    f32, bf16 = jnp.float32, jnp.bfloat16
    dma = pltpu.SemaphoreType.DMA
    vmem = pl.BlockSpec(memory_space=pltpu.VMEM)
    smem = pl.BlockSpec(memory_space=pltpu.SMEM)
    out = pl.pallas_call(
        functools.partial(body, C, T, rows),
        out_shape=jax.ShapeDtypeStruct((STEPS * VS, rows, LAGS // T), f32),
        in_specs=[smem, smem, smem, vmem],
        out_specs=vmem,
        scratch_shapes=[
            pltpu.VMEM((rows, LANES), bf16),
            pltpu.VMEM((rows, samples), f32),
            pltpu.VMEM((rows, samples), f32),
            pltpu.VMEM((T, rows, LANES), f32),
            pltpu.VMEM((C, rows, samples), bf16),
            pltpu.VMEM((T, rows, samples), bf16),
            pltpu.VMEM((T, rows, samples), bf16),
            pltpu.VMEM((rows, LANES + T * samples), f32),
            pltpu.VMEM((rows, T * samples + LAGS + LANES), f32),
            dma, dma, dma, dma,
            dma((T,)), dma((T,)), dma((C,)), dma((C,)),
            dma((T,)), dma((T,)), dma((T,)), dma((T,)),
        ],
        compiler_params=pltpu.CompilerParams(
            collective_id=0, has_side_effects=True, vmem_limit_bytes=32 * 2**20),
        cost_estimate=pl.CostEstimate(flops=600_000_000, bytes_accessed=1_000_000, transcendentals=0),
    )(fir_taps, pair_rows, source_blocks, records)
    return out.reshape(STEPS, VS, rows, LAGS // T)


def solution(mesh):
    return jax.shard_map(
        shards,
        mesh=mesh,
        in_specs=(P("chan", "tm"), P("chan", None), P(), P()),
        out_specs=P(None, None, "chan", "tm"),
        check_vma=False,
    )
```

time: 770 us -> 31.9 us (0.04); the launches traced: 759 us -> 31.7 us
  local copies, waits for them, and re-layouts: 624 us -> 3.57 us
  blocking collectives: 32.3 us -> 0 us
  Pallas kernels: 0 us -> 28.1 us
  waiting for transfers between devices: 27.1 us -> 0 us
  other arithmetic: 25.5 us -> 0 us
  matrix products: 21.1 us -> 0 us
  between operations: 20.7 us -> 0.01 us
  starting transfers between devices: 8.97 us -> 0 us
    unnamed x1970 -> x9, local copies, waits for them, and re-layouts: 460 us -> 3.57 us
    slice x36 -> x0, local copies, waits for them, and re-layouts: 77.3 us -> none  [the longest x32 71.9 us: shards(): extended[:, begin:begin + 4 * samples:4]]
    another operation x145 -> x0, local copies, waits for them, and re-layouts: 76.1 us -> none  [the longest x144 76.1 us: skewed_tile(): return jnp.stack(shifted, axis=1)]
    psum x2 -> x0, blocking collectives: 32.3 us -> none  [the longest x1 22.4 us: broadcast(): return lax.psum(block, axis)]
    pallas_call x0 -> x1, Pallas kernels: none -> 28.1 us  [shards(): pl.pallas_call(functools.partial(body, C, T, rows), out_shape=jax.ShapeDt...]
    reduce_scatter x1 -> x0, waiting for transfers between devices: 25.4 us -> none  [shards(): lax.psum_scatter(partial_stacks, 'tm', scatter_dimension=3, tiled=True)]
    dot_general x16 -> x0, matrix products: 21.1 us -> none  [one_segment(): jnp.einsum('cu,rku->rck', receiver, tile_rows, preferred_element_type=jnp...]
    reduce_sum x1 -> x0, other arithmetic: 20.2 us -> none  [shards(): row_total = lax.psum(jnp.sum(filtered * filtered, axis=1), 'tm')]
  transfers between devices with their start and end apart: 4 -> 0, of which waited for: 2 -> 0; matrix products, arithmetic and copies ran while one was open for 2% -> 0% of each run, Pallas kernels for 0% -> 0%
where the time goes in v1:
time: 31.9 us; the launch traced here: 31.7 us
  Pallas kernels  28.1 us (88%)
  local copies, waits for them, and re-layouts  3.57 us (11%)
    pallas_call x1, Pallas kernels, shards(): pl.pallas_call(functools.partial(body, C, T, rows), out_shape=jax.ShapeDt...  28.1 us
    unnamed x9, local copies, waits for them, and re-layouts  3.57 us

profile of v1, /device:TPU:0, one launch (start us, length us, event | category | flops | bytes accessed | tf_op | source)
XLA Modules:
  0.0 31.7 jit_solution(13652768433616871622)
XLA Ops:
  0.0 0.0 copy-start
  0.0 0.9 %copy-done = bf16[16,4096]{1,0:T(8,128)(2,1)S(1)} copy-done((bf16[16,4096]{1,0:T(8,128)(2,1)S(1)}, bf16[16,4096]{1,0:T(8,128)(2,1)}, u32[]{:S(2)}) %copy-start) | copy-done | bytes 131096
  0.9 0.0 copy-start.1
  0.9 0.7 %copy-done.1 = f32[32]{0:T(128)S(1)} copy-done((f32[32]{0:T(128)S(1)}, f32[32]{0:T(128)}, u32[]{:S(2)}) %copy-start.1) | copy-done | bytes 152
  1.6 0.0 copy-start.2
  1.6 0.7 %copy-done.2 = s32[1,16]{1,0:T(1,128)S(1)} copy-done((s32[1,16]{1,0:T(1,128)S(1)}, s32[1,16]{1,0:T(1,128)}, u32[]{:S(2)}) %copy-start.2) | copy-done | bytes 88
  2.2 0.0 copy-start.3
  2.2 0.7 %copy-done.3 = s32[2]{0:T(128)S(1)} copy-done((s32[2]{0:T(128)S(1)}, s32[2]{0:T(128)}, u32[]{:S(2)}) %copy-start.3) | copy-done | bytes 32
  2.9 28.1 %shard_map.46 = f32[16,16,256]{2,1,0:T(8,128)S(1)} custom-call(f32[32]{0:T(128)S(1)} %copy-done.1, s32[1,16]{1,0:T(1,128)S(1)} %copy-done.2, s32[2]{0:T(128)S(1)} %copy-done.3, bf16[16,4096]{1,0:T(8,128)(2,1)S(1)} %copy-done), custom_call_target="tpu_custom_call" | custom-call | flops 600000000 | bytes 1000000 | tf_op jit(solution)/shard_map/pallas_call | solution.py:211
  31.0 0.7 %copy.6 = f32[2,8,16,256]{3,2,1,0:T(8,128)} copy(f32[2,8,16,256]{3,2,1,0:T(8,128)S(1)} %bitcast.1) | data formatting | bytes 524288
Async XLA Ops:
  0.0 0.9 %copy-start = (bf16[16,4096]{1,0:T(8,128)(2,1)S(1)}, bf16[16,4096]{1,0:T(8,128)(2,1)}, u32[]{:S(2)}) copy-start(bf16[16,4096]{1,0:T(8,128)(2,1)} %rec_ref.1) | copy-start | bytes 393220
  0.9 0.7 %copy-start.1 = (f32[32]{0:T(128)S(1)}, f32[32]{0:T(128)}, u32[]{:S(2)}) copy-start(f32[32]{0:T(128)} %taps_ref.1) | copy-start | bytes 388
  1.6 0.7 %copy-start.2 = (s32[1,16]{1,0:T(1,128)S(1)}, s32[1,16]{1,0:T(1,128)}, u32[]{:S(2)}) copy-start(s32[1,16]{1,0:T(1,128)} %pair_ref.1) | copy-start | bytes 196
  2.2 0.7 %copy-start.3 = (s32[2]{0:T(128)S(1)}, s32[2]{0:T(128)}, u32[]{:S(2)}) copy-start(s32[2]{0:T(128)} %blocks_ref.1) | copy-start | bytes 28

commit v2 on v1

--- a/solution.py
+++ b/solution.py
@@ -16,8 +16,9 @@
 FINE = 16
 
 
-def body(C, T, rows, taps_ref, pair_ref, blocks_ref, rec_ref, out_ref,
-         halo, filt, pfilt, pw, chw, tw, ts, sp, wp,
+def body(C, T, rows, taps_hbm, pair_hbm, blocks_hbm, rec_hbm, out_ref,
+         taps_ref, pair_ref, blocks_ref, rec_ref, local_s,
+         halo, filt, pfilt, pw, chw, tw, ts, wp, wall,
          halo_s, halo_r, part_s, part_r, pw_s, pw_r, ch_s, ch_r, tw_s, tw_r, ts_s, ts_r):
     me = lax.axis_index("chan")
     t = lax.axis_index("tm")
@@ -34,6 +35,10 @@
     def at_tm(d):
         return lax.rem(t + d, T)
 
+    loads = [pltpu.make_async_copy(src, dst, local_s.at[i]) for i, (src, dst) in enumerate((
+        (taps_hbm, taps_ref), (rec_hbm, rec_ref), (pair_hbm, pair_ref), (blocks_hbm, blocks_ref)))]
+    for load in loads:
+        load.start()
     barrier = pltpu.get_barrier_semaphore()
     for d in range(1, C):
         pl.semaphore_signal(barrier, inc=1, device_id={"chan": at_chan(d)}, device_id_type=pl.DeviceIdType.MESH)
@@ -51,18 +56,20 @@
     n = lax.broadcasted_iota(jnp.int32, (depth, LANES), 1)
     tap = 4 * n + 3 - (j - LANES)
     band = jnp.zeros((depth, LANES), f32)
+    loads[0].wait()
     for k in range(TAPS):
         band = jnp.where(tap == k, taps_ref[k], band)
     hi = band.astype(bf16)
     lo = (band - hi.astype(f32)).astype(bf16)
     band2 = jnp.concatenate([hi, lo], axis=1)
 
+    for load in loads[1:]:
+        load.wait()
     pl.semaphore_wait(barrier, C + T - 2)
     tail = rec_ref.shape[1] - LANES
     halo_copy = remote(rec_ref.at[:, pl.ds(tail, LANES)], halo, halo_s, halo_r, {"tm": at_tm(1)})
     halo_copy.start()
 
-    sp[:, :LANES] = jnp.zeros((rows, LANES), f32)
     wp[:, window:] = jnp.zeros((rows, wp.shape[1] - window), f32)
 
     groups = samples // LANES
@@ -143,9 +150,6 @@
     arrive(tw, tw_s, tw_r, T, "tm", at_tm)
     for i in range(T):
         wp[:, samples * i:samples * (i + 1)] = tw[i].astype(f32)
-    arrive(ts, ts_s, ts_r, T, "tm", at_tm)
-    for i in range(T):
-        sp[:, LANES + samples * i:LANES + samples * (i + 1)] = ts[i].astype(f32)
 
     lag0 = t * lag_dev
     wide = samples + LANES * P_
@@ -155,28 +159,37 @@
         base = lax.div(lag0, LANES) * LANES
         rest = lax.rem(lag0, LANES)
 
-    def block(i, z):
-        s0 = pl.multiple_of(i * samples, LANES)
-        w0 = pl.multiple_of(i * samples + base, LANES)
-        srows = sp[:, pl.ds(s0, samples + LANES)]
-        wrows = wp[:, pl.ds(w0, wide)]
+    for i in range(T):
+        wrows = wp[:, pl.ds(pl.multiple_of(i * samples + base, LANES), wide)]
+        for a in range(A_):
+            rolled = wrows
+            if lag_dev % LANES:
+                rolled = pltpu.roll(wrows, wide - FINE * a - rest, 1)
+            elif a:
+                rolled = pltpu.roll(wrows, wide - FINE * a, 1)
+            for p in range(P_):
+                r0 = (p * A_ + a) * rows
+                wall[r0:r0 + rows, samples * i:samples * (i + 1)] = (
+                    rolled[:, LANES * p:LANES * p + samples].astype(bf16))
+    wall[:, window:] = jnp.zeros((wall.shape[0], LANES), bf16)
+
+    span = samples + LANES
+
+    def term(slot):
+        srows = jnp.concatenate([ts[slot].astype(f32), jnp.zeros((rows, LANES), f32)], axis=1)
         xs = []
         for s in range(STEPS * VS):
-            one = jnp.broadcast_to(srows[s:s + 1], (FINE, samples + LANES))
-            xs.append(pltpu.roll(one, 0, 1, stride=1, stride_axis=0)[:, LANES:].astype(bf16))
-        rolled = []
-        for a in range(A_):
-            if lag_dev % LANES == 0:
-                sh = (wide - FINE * a) % wide
-            else:
-                sh = wide - FINE * a - rest
-            rolled.append(pltpu.roll(wrows, sh, 1) if not (isinstance(sh, int) and sh == 0) else wrows)
-        ws = [rolled[a][:, LANES * p:LANES * p + samples].astype(bf16)
-              for p in range(P_) for a in range(A_)]
-        return z + lax.dot_general(jnp.concatenate(ws, axis=0), jnp.concatenate(xs, axis=0),
-                                   (((1,), (1,)), ((), ())), preferred_element_type=f32)
-
-    z = lax.fori_loop(0, T, block, jnp.zeros((P_ * A_ * rows, STEPS * VS * FINE), f32))
+            one = jnp.broadcast_to(srows[s:s + 1], (FINE, span))
+            xs.append(pltpu.roll(one, 0, 1, stride=1, stride_axis=0).astype(bf16))
+        ws = wall[:, pl.ds(pl.multiple_of(slot * samples, LANES), span)]
+        return lax.dot_general(ws, jnp.concatenate(xs, axis=0),
+                               (((1,), (1,)), ((), ())), preferred_element_type=f32)
+
+    z = term(t)
+    for d in range(1, T):
+        slot = at_tm(T - d)
+        remote(ts.at[slot], ts.at[slot], ts_s.at[d], ts_r.at[d], {"tm": at_tm(d)}).wait_recv()
+        z = z + term(slot)
     z = z * (1.0 / math.sqrt(window))
 
     lane_group = lax.broadcasted_iota(jnp.int32, (rows, LANES), 1) // FINE
@@ -207,13 +220,18 @@
     f32, bf16 = jnp.float32, jnp.bfloat16
     dma = pltpu.SemaphoreType.DMA
     vmem = pl.BlockSpec(memory_space=pltpu.VMEM)
-    smem = pl.BlockSpec(memory_space=pltpu.SMEM)
+    hbm = pl.BlockSpec(memory_space=pltpu.HBM)
     out = pl.pallas_call(
         functools.partial(body, C, T, rows),
         out_shape=jax.ShapeDtypeStruct((STEPS * VS, rows, LAGS // T), f32),
-        in_specs=[smem, smem, smem, vmem],
+        in_specs=[hbm] * 4,
         out_specs=vmem,
         scratch_shapes=[
+            pltpu.SMEM(fir_taps.shape, f32),
+            pltpu.SMEM(pair_rows.shape, jnp.int32),
+            pltpu.SMEM(source_blocks.shape, jnp.int32),
+            pltpu.VMEM(records.shape, bf16),
+            dma((4,)),
             pltpu.VMEM((rows, LANES), bf16),
             pltpu.VMEM((rows, samples), f32),
             pltpu.VMEM((rows, samples), f32),
@@ -221,14 +239,14 @@
             pltpu.VMEM((C, rows, samples), bf16),
             pltpu.VMEM((T, rows, samples), bf16),
             pltpu.VMEM((T, rows, samples), bf16),
-            pltpu.VMEM((rows, LANES + T * samples), f32),
             pltpu.VMEM((rows, T * samples + LAGS + LANES), f32),
+            pltpu.VMEM((LAGS // T // FINE * rows, T * samples + LANES), bf16),
             dma, dma, dma, dma,
             dma((T,)), dma((T,)), dma((C,)), dma((C,)),
             dma((T,)), dma((T,)), dma((T,)), dma((T,)),
         ],
         compiler_params=pltpu.CompilerParams(
-            collective_id=0, has_side_effects=True, vmem_limit_bytes=32 * 2**20),
+            collective_id=0, has_side_effects=True, vmem_limit_bytes=60 * 2**20),
         cost_estimate=pl.CostEstimate(flops=600_000_000, bytes_accessed=1_000_000, transcendentals=0),
     )(fir_taps, pair_rows, source_blocks, records)
     return out.reshape(STEPS, VS, rows, LAGS // T)

time: 31.9 us -> 29.9 us (0.937)
  local copies, waits for them, and re-layouts: 3.57 us -> 1.67 us
    unnamed x9 -> x1, local copies, waits for them, and re-layouts: 3.57 us -> 1.67 us
where the time goes in v2:
time: 29.9 us; the launch traced here: 29.7 us
  Pallas kernels  28.1 us (94%)
  local copies, waits for them, and re-layouts  1.67 us (6%)
    pallas_call x1, Pallas kernels, shards(): pl.pallas_call(functools.partial(body, C, T, rows), out_shape=jax.ShapeDt...  28.1 us
    unnamed x1, local copies, waits for them, and re-layouts  1.67 us

profile of v2, /device:TPU:0, one launch (start us, length us, event | category | flops | bytes accessed | tf_op | source)
XLA Modules:
  0.0 29.7 jit_solution(9519257156934979004)
XLA Ops:
  0.0 28.1 %shard_map.46 = f32[16,16,256]{2,1,0:T(8,128)} custom-call(f32[32]{0:T(128)} %taps_hbm.1, s32[1,16]{1,0:T(1,128)} %pair_hbm.1, s32[2]{0:T(128)} %blocks_hbm.1, bf16[16,4096]{1,0:T(8,128)(2,1)} %rec_hbm.1), custom_call_target="tpu_custom_call" | custom-call | flops 600000000 | bytes 1000000 | tf_op jit(solution)/shard_map/pallas_call | solution.py:224
  28.1 1.7 %copy.6 = f32[2,8,16,256]{3,2,1,0:T(8,128)} copy(f32[2,8,16,256]{3,2,1,0:T(8,128)} %bitcast.1) | data formatting | bytes 524288

commit v3 on v2

--- a/solution.py
+++ b/solution.py
@@ -18,8 +18,8 @@
 
 def body(C, T, rows, taps_hbm, pair_hbm, blocks_hbm, rec_hbm, out_ref,
          taps_ref, pair_ref, blocks_ref, rec_ref, local_s,
-         halo, filt, pfilt, pw, chw, tw, ts, wp, wall,
-         halo_s, halo_r, part_s, part_r, pw_s, pw_r, ch_s, ch_r, tw_s, tw_r, ts_s, ts_r):
+         halo, phalo, praw, pw, chw, tw, ts, wp, wall,
+         halo_s, halo_r, phalo_s, phalo_r, part_s, part_r, pw_s, pw_r, ch_s, ch_r, tw_s, tw_r, ts_s, ts_r):
     me = lax.axis_index("chan")
     t = lax.axis_index("tm")
     f32, bf16 = jnp.float32, jnp.bfloat16
@@ -44,6 +44,9 @@
         pl.semaphore_signal(barrier, inc=1, device_id={"chan": at_chan(d)}, device_id_type=pl.DeviceIdType.MESH)
     for d in range(1, T):
         pl.semaphore_signal(barrier, inc=1, device_id={"tm": at_tm(d)}, device_id_type=pl.DeviceIdType.MESH)
+
+    pl.semaphore_signal(barrier, inc=1, device_id={"chan": at_chan(C // 2), "tm": at_tm(T - 1)},
+                        device_id_type=pl.DeviceIdType.MESH)
 
     def remote(src, dst, ssem, rsem, where):
         return pltpu.make_async_remote_copy(
@@ -65,44 +68,53 @@
 
     for load in loads[1:]:
         load.wait()
-    pl.semaphore_wait(barrier, C + T - 2)
+    pl.semaphore_wait(barrier, C + T - 1)
     tail = rec_ref.shape[1] - LANES
-    halo_copy = remote(rec_ref.at[:, pl.ds(tail, LANES)], halo, halo_s, halo_r, {"tm": at_tm(1)})
+    last = rec_ref.at[:, pl.ds(tail, LANES)]
+    phalo_copy = remote(last, phalo, phalo_s, phalo_r, {"chan": at_chan(C // 2), "tm": at_tm(1)})
+    halo_copy = remote(last, halo, halo_s, halo_r, {"tm": at_tm(1)})
+    part_copy = remote(rec_ref, praw, part_s, part_r, {"chan": at_chan(C // 2)})
+    phalo_copy.start()
     halo_copy.start()
+    part_copy.start()
 
     wp[:, window:] = jnp.zeros((rows, wp.shape[1] - window), f32)
-
-    groups = samples // LANES
-    parts = []
-    for g in range(groups):
-        if g == 0:
-            first = jnp.zeros((rows, LANES), bf16)
-        else:
-            first = rec_ref[:, group * g - LANES:group * g]
-        parts.append(jnp.concatenate([first, rec_ref[:, group * g:group * (g + 1)]], axis=1))
-    lhs = jnp.concatenate(parts, axis=0)
-    both = jnp.dot(lhs, band2, preferred_element_type=f32)
-    res = both[:, :LANES] + both[:, LANES:]
-    halo_copy.wait()
-    edge = jnp.dot(halo[...], band2[:LANES], preferred_element_type=f32)
-    edge = edge[:, :LANES] + edge[:, LANES:]
-    edge = jnp.where(t > 0, edge, jnp.zeros_like(edge))
-    for g in range(groups):
-        piece = res[rows * g:rows * (g + 1)]
-        if g == 0:
-            piece = piece + edge
-        filt[:, LANES * g:LANES * (g + 1)] = piece
-    part_copy = remote(filt, pfilt, part_s, part_r, {"chan": at_chan(C // 2)})
-    part_copy.start()
+    wall[:, window:] = jnp.zeros((wall.shape[0], LANES), bf16)
     rr = lax.broadcasted_iota(jnp.int32, (rows, rows), 0)
     cc = lax.broadcasted_iota(jnp.int32, (rows, rows), 1)
     pick = jnp.zeros((rows, rows), jnp.int32)
     for r in range(rows):
         pick = jnp.where(rr == r, pair_ref[0, r], pick)
-    perm = jnp.where(pick == cc, 1.0, 0.0).astype(f32)
+    perm = jnp.where(pick == cc, 1.0, 0.0).astype(bf16)
+
+    groups = samples // LANES
+
+    def filter_rows(raw):
+        parts = []
+        for g in range(groups):
+            if g == 0:
+                first = jnp.zeros((rows, LANES), bf16)
+            else:
+                first = raw[:, group * g - LANES:group * g]
+            parts.append(jnp.concatenate([first, raw[:, group * g:group * (g + 1)]], axis=1))
+        both = jnp.dot(jnp.concatenate(parts, axis=0), band2, preferred_element_type=f32)
+        return both[:, :LANES] + both[:, LANES:]
+
+    def permuted(x):
+        return jnp.dot(perm, x, preferred_element_type=f32).astype(bf16)
+
+    own = filter_rows(rec_ref[...])
+    phalo_copy.wait()
+    halo_copy.wait()
+    edges = jnp.concatenate([halo[...], permuted(phalo[...])], axis=0)
+    edges = jnp.dot(edges, band2[:LANES], preferred_element_type=f32)
+    edges = edges[:, :LANES] + edges[:, LANES:]
+    edge = edges[:rows] + edges[rows:]
+    edge = jnp.where(t > 0, edge, jnp.zeros_like(edge))
     part_copy.wait()
-    filtered = 0.5 * (filt[...] + jnp.dot(perm, pfilt[...], precision=lax.Precision.HIGHEST,
-                                          preferred_element_type=f32))
+    res = own + filter_rows(permuted(praw[...]))
+    filtered = 0.5 * jnp.concatenate(
+        [res[:rows] + edge] + [res[rows * g:rows * (g + 1)] for g in range(1, groups)], axis=1)
     sq = filtered * filtered
     acc = sq[:, :LANES]
     for g in range(1, groups):
@@ -171,7 +183,6 @@
                 r0 = (p * A_ + a) * rows
                 wall[r0:r0 + rows, samples * i:samples * (i + 1)] = (
                     rolled[:, LANES * p:LANES * p + samples].astype(bf16))
-    wall[:, window:] = jnp.zeros((wall.shape[0], LANES), bf16)
 
     span = samples + LANES
 
@@ -196,17 +207,19 @@
     per_tile = LANES // FINE
     width = min(lag_dev, LANES)
     for p in range(P_):
-        for s in range(STEPS * VS):
-            lo_s = s // per_tile * LANES
-            o = None
+        for lo_s in range(0, STEPS * VS, per_tile):
+            turned = []
             for a in range(A_):
                 r0 = (p * A_ + a) * rows
-                tile = z[r0:r0 + rows, lo_s:lo_s + LANES]
-                sh = (FINE * (a - s % per_tile)) % LANES
-                if sh:
-                    tile = pltpu.roll(tile, sh, 1)
-                o = tile if o is None else jnp.where(lane_group == a, tile, o)
-            out_ref[s, :, LANES * p:LANES * p + width] = o[:, :width]
+                tile = z[r0:r0 + rows, lo_s * FINE:lo_s * FINE + LANES]
+                turned.append(pltpu.roll(tile, FINE * a, 1) if a else tile)
+            for s in range(per_tile):
+                o = turned[0]
+                for a in range(1, A_):
+                    o = jnp.where(lane_group == (s + a) % per_tile, turned[a], o)
+                if s:
+                    o = pltpu.roll(o, LANES - FINE * s, 1)
+                out_ref[lo_s + s, :, LANES * p:LANES * p + width] = o[:, :width]
 
     for s in pw_sends + ch_sends + tw_sends + ts_sends:
         s.wait_send()
@@ -233,15 +246,15 @@
             pltpu.VMEM(records.shape, bf16),
             dma((4,)),
             pltpu.VMEM((rows, LANES), bf16),
-            pltpu.VMEM((rows, samples), f32),
-            pltpu.VMEM((rows, samples), f32),
+            pltpu.VMEM((rows, LANES), bf16),
+            pltpu.VMEM((rows, raw), bf16),
             pltpu.VMEM((T, rows, LANES), f32),
             pltpu.VMEM((C, rows, samples), bf16),
             pltpu.VMEM((T, rows, samples), bf16),
             pltpu.VMEM((T, rows, samples), bf16),
             pltpu.VMEM((rows, T * samples + LAGS + LANES), f32),
             pltpu.VMEM((LAGS // T // FINE * rows, T * samples + LANES), bf16),
-            dma, dma, dma, dma,
+            dma, dma, dma, dma, dma, dma,
             dma((T,)), dma((T,)), dma((C,)), dma((C,)),
             dma((T,)), dma((T,)), dma((T,)), dma((T,)),
         ],

time: 29.9 us -> 27.5 us (0.920)
  Pallas kernels: 28.1 us -> 25.7 us
    pallas_call x1, Pallas kernels: 28.1 us -> 25.7 us  [shards(): pl.pallas_call(functools.partial(body, C, T, rows), out_shape=jax.ShapeDt...]
where the time goes in v3:
time: 27.5 us; the launch traced here: 27.4 us
  Pallas kernels  25.7 us (93%)
  local copies, waits for them, and re-layouts  1.67 us (6%)
    pallas_call x1, Pallas kernels, shards(): pl.pallas_call(functools.partial(body, C, T, rows), out_shape=jax.ShapeDt...  25.7 us
    unnamed x1, local copies, waits for them, and re-layouts  1.67 us

profile of v3, /device:TPU:0, one launch (start us, length us, event | category | flops | bytes accessed | tf_op | source)
XLA Modules:
  0.0 27.4 jit_solution(14125992276805342990)
XLA Ops:
  0.0 25.7 %shard_map.46 = f32[16,16,256]{2,1,0:T(8,128)} custom-call(f32[32]{0:T(128)} %taps_hbm.1, s32[1,16]{1,0:T(1,128)} %pair_hbm.1, s32[2]{0:T(128)} %blocks_hbm.1, bf16[16,4096]{1,0:T(8,128)(2,1)} %rec_hbm.1), custom_call_target="tpu_custom_call" | custom-call | flops 600000000 | bytes 1000000 | tf_op jit(solution)/shard_map/pallas_call | solution.py:237
  25.7 1.7 %copy.6 = f32[2,8,16,256]{3,2,1,0:T(8,128)} copy(f32[2,8,16,256]{3,2,1,0:T(8,128)} %bitcast.1) | data formatting | bytes 524288

commit v4 on v3

--- a/solution.py
+++ b/solution.py
@@ -197,8 +197,12 @@
                                (((1,), (1,)), ((), ())), preferred_element_type=f32)
 
     z = term(t)
-    for d in range(1, T):
-        slot = at_tm(T - d)
+    low = t < T // 2
+    edge_dist = jnp.where(low, t, T - 1 - t)
+    for k in range(T - 1):
+        up = jnp.where(k >= edge_dist, k + 1, k)
+        slot = jnp.where(low, up, T - 1 - up)
+        d = lax.rem(t - slot + T, T)
         remote(ts.at[slot], ts.at[slot], ts_s.at[d], ts_r.at[d], {"tm": at_tm(d)}).wait_recv()
         z = z + term(slot)
     z = z * (1.0 / math.sqrt(window))

time: 27.5 us -> 26.4 us (0.960)
  Pallas kernels: 25.7 us -> 24.6 us
    pallas_call x1, Pallas kernels: 25.7 us -> 24.6 us  [shards(): pl.pallas_call(functools.partial(body, C, T, rows), out_shape=jax.ShapeDt...]
where the time goes in v4:
time: 26.4 us; the launch traced here: 26.3 us
  Pallas kernels  24.6 us (93%)
  local copies, waits for them, and re-layouts  1.67 us (6%)
    pallas_call x1, Pallas kernels, shards(): pl.pallas_call(functools.partial(body, C, T, rows), out_shape=jax.ShapeDt...  24.6 us
    unnamed x1, local copies, waits for them, and re-layouts  1.67 us

profile of v4, /device:TPU:0, one launch (start us, length us, event | category | flops | bytes accessed | tf_op | source)
XLA Modules:
  0.0 26.3 jit_solution(18318130670474948709)
XLA Ops:
  0.0 24.6 %shard_map.46 = f32[16,16,256]{2,1,0:T(8,128)} custom-call(f32[32]{0:T(128)} %taps_hbm.1, s32[1,16]{1,0:T(1,128)} %pair_hbm.1, s32[2]{0:T(128)} %blocks_hbm.1, bf16[16,4096]{1,0:T(8,128)(2,1)} %rec_hbm.1), custom_call_target="tpu_custom_call" | custom-call | flops 600000000 | bytes 1000000 | tf_op jit(solution)/shard_map/pallas_call | solution.py:241
  24.6 1.7 %copy.6 = f32[2,8,16,256]{3,2,1,0:T(8,128)} copy(f32[2,8,16,256]{3,2,1,0:T(8,128)} %bitcast.1) | data formatting | bytes 524288
